TPU v7x, 128 devices: a whole 4x4x4 slice. The times are simulated.
128 devices in a mesh: dom: 32 (over z, x, core), sub: 4 (over y).
Axes of the slice: x: 4, y: 4, z: 4, core: 2. Of those that a mesh axis runs over, the one named last changes fastest.
Arguments:
- start_block: bfloat16 [64, 524288], P(None, ('dom', 'sub')), may hold values from -6 to 6
- tiles_in: bfloat16 [4096, 12, 128, 128], P(('dom', 'sub')), may hold values from -86 to 86, as said below
- tiles_out: bfloat16 [4096, 4, 128, 128], P(('dom', 'sub')), may hold values from -86 to 86, as said below
- in_cols: int32 [4096, 12], P(('dom', 'sub')), may hold values from 0 to 127
- out_cols: int32 [4096, 4], P(('dom', 'sub')), may hold values from 0 to 127
- export_list: int32 [32, 4, 4], P('dom', 'sub'), may hold values from 0 to 127
- recv_list: int32 [32, 4, 32, 4], P('dom', 'sub'), may hold values from 0 to 3
Outputs:
- basis: float32 [64, 524288], P(None, ('dom', 'sub'))
- projected: float32 [64, 64], replicated
Inputs may be any that keep to these rules, and one draw needn't show every extreme that they name: `tiles_in`: tile weights; row magnitudes differ over the graph. `tiles_out`: laid out as tiles_in, with the same row magnitudes.
All inputs are finite; a program needn't handle non-finite values.
Results may differ from a plain program's by a relative error of at most 0.0057.
Values may be sent and summed in bfloat16 or wider, within the bound.
A program may use at most 128 MiB of HBM per device.

v0:
```python
import math

import jax
import jax.numpy as jnp
from jax import lax
from jax.sharding import PartitionSpec as P


def body(start_block, tiles_in, tiles_out, in_cols, out_cols, export_list, recv_list):
    dom_size = lax.axis_size("dom")
    sub_size = lax.axis_size("sub")
    width, local_rows = start_block.shape
    tile_size = tiles_in.shape[-1]
    local_blocks = tiles_in.shape[0]
    capacity = recv_list.shape[-1]
    offered = export_list.shape[-1]
    exports = export_list.reshape(offered)
    requested = recv_list.reshape(dom_size, capacity)
    count = (tiles_in.shape[1] + tiles_out.shape[1]) * tile_size
    magnitude = (
        jnp.sum(jnp.abs(tiles_in), axis=(1, 2), dtype=jnp.float32)
        + jnp.sum(jnp.abs(tiles_out), axis=(1, 2), dtype=jnp.float32)
    ) / count + 1e-06
    inverse_root = (1.0 / jnp.sqrt(magnitude)).reshape(local_rows)
    spectral = 1.0 / (1.25 * math.sqrt(count))
    row_factor = (spectral * inverse_root)[None, :]
    wanted = exports[lax.all_to_all(requested, "dom", split_axis=0, concat_axis=0, tiled=True)]

    def fetch(partition):
        outgoing = partition[:, wanted, :]
        incoming = lax.all_to_all(outgoing, "dom", split_axis=1, concat_axis=1, tiled=True)
        return incoming.reshape(width, dom_size * capacity, tile_size)

    def operate(vectors):
        scaled = (
            (vectors * inverse_root[None, :])
            .astype(jnp.bfloat16)
            .reshape(width, local_blocks, tile_size)
        )
        partition = lax.all_gather(scaled, "sub", axis=1, tiled=True)
        remote = fetch(partition)
        inner = jnp.einsum(
            "kbpc,bpcr->kbr", partition[:, in_cols], tiles_in, preferred_element_type=jnp.float32
        )
        outer = jnp.einsum(
            "kbpc,bpcr->kbr", remote[:, out_cols], tiles_out, preferred_element_type=jnp.float32
        )
        return (inner + outer).reshape(width, local_rows) * row_factor

    first = start_block.astype(jnp.float32)
    second = operate(first)
    third = 2.0 * operate(second) - first
    filtered = 2.0 * operate(third) - second
    rows_total = local_rows * dom_size * sub_size
    gram_local = jnp.dot(filtered, filtered.T, precision=lax.Precision.HIGHEST)
    image = operate(filtered)
    rayleigh_local = jnp.dot(filtered, image.T, precision=lax.Precision.HIGHEST)
    gram_total, rayleigh_total = lax.psum((gram_local, rayleigh_local), ("dom", "sub"))
    gram = gram_total / rows_total
    rayleigh = rayleigh_total / rows_total
    lower = jnp.linalg.cholesky(gram)
    basis = jax.scipy.linalg.solve_triangular(lower, filtered, lower=True)
    halfway = jax.scipy.linalg.solve_triangular(lower, rayleigh, lower=True)
    projected = jax.scipy.linalg.solve_triangular(lower, halfway.T, lower=True).T
    return (basis, projected)


def solution(mesh):
    return jax.shard_map(
        body,
        mesh=mesh,
        in_specs=(
            P(None, ("dom", "sub")),
            P(("dom", "sub"), None, None, None),
            P(("dom", "sub"), None, None, None),
            P(("dom", "sub"), None),
            P(("dom", "sub"), None),
            P("dom", "sub", None),
            P("dom", "sub", None, None),
        ),
        out_specs=(P(None, ("dom", "sub")), P()),
        check_vma=False,
    )
```

profile of v0, /device:TPU:1, one launch (start us, length us, event | category | flops | bytes accessed | tf_op | source)
XLA Modules:
  0.0 412.5 jit_solution(10347095565075736180)
XLA Ops:
  7.2 7.8 %convert_reduce_fusion = f32[32,128]{1,0:T(8,128)S(1)} fusion(bf16[32,12,128,128]{3,2,1,0:T(8,128)(2,1)} %param.10), kind=kLoop, calls=%fused_computation.12 | loop fusion | flops 18870272 | bytes 12599296 | tf_op jit(solution)/shard_map/reduce_sum | solution.py:21
  15.1 0.9 convert_reduce_fusion.1
  16.0 0.1 copy-done.7
  16.1 0.9 copy_bitcast_fusion.1
  17.0 0.7 copy.37
  17.7 9.4 %all-to-all-start = ((s32[32,1,4]{2,1,0:T(1,128)}), s32[32,1,4]{2,1,0:T(1,128)S(1)}, u32[]{:S(2)}, u32[]{:S(2)}) async-start(s32[32,1,4]{2,1,0:T(1,128)} %copy.37), calls=%async_computation | async-start | bytes 32768 | tf_op jit(solution)/shard_map/all_to_all | solution.py:27
  27.2 0.7 fusion.32
  27.9 6.2 %all-to-all-done = s32[32,1,4]{2,1,0:T(1,128)S(1)} async-done(((s32[32,1,4]{2,1,0:T(1,128)}), s32[32,1,4]{2,1,0:T(1,128)S(1)}, u32[]{:S(2)}, u32[]{:S(2)}) %all-to-all-start) | async-done | bytes 544 | tf_op jit(solution)/shard_map/all_to_all | solution.py:27
  34.1 2.6 compare_select_fusion.2
  36.7 0.1 copy.39
  36.8 0.1 reshape.223
  36.9 14.3 %all-gather.5.cloned.1.call-done = bf16[64,128,128]{2,0,1:T(8,128)(2,1)} async-done(((bf16[64,32,128]{2,0,1:T(8,128)(2,1)}), bf16[64,128,128]{2,0,1:T(8,128)(2,1)}) %all-gather.5.cloned.1.call-update) | async-done | bytes 2097168 | tf_op jit(solution)/shard_map/all_gather | solution.py:40
  51.3 3.8 gather_fusion.1
  55.1 7.9 %all-to-all-start.1 = ((bf16[64,32,4,128]{3,0,2,1:T(8,128)(2,1)}), bf16[64,32,4,128]{3,0,2,1:T(8,128)(2,1)}, u32[]{:S(2)}, u32[]{:S(2)}) async-start(bf16[64,32,4,128]{3,0,2,1:T(8,128)(2,1)} %bitcast.188), calls=%async_computation.1 | async-start | bytes 4194304 | tf_op jit(solution)/shard_map/all_to_all | solution.py:31
  62.9 0.6 all-gather.7.cloned.1.call-start
  63.5 0.1 copy.36
  63.6 0.1 reshape.204
  63.7 0.1 copy.40
  63.8 0.1 reshape.231
  64.0 13.3 %gather_fusion = bf16[384,64,128]{2,1,0:T(8,128)(2,1)} fusion(bf16[64,128,128]{2,0,1:T(8,128)(2,1)S(1)} %copy-done.1, s32[1024]{0:T(1024)S(1)} %pad_clamp_fusion.2), kind=kCustom, calls=%fused_computation | custom fusion | bytes 12584448 | tf_op jit(solution)/shard_map/gather | solution.py:43
  77.3 9.0 %convolution_bitcast_fusion.7 = f32[32,64,128]{2,1,0:T(8,128)S(1)} fusion(bf16[64,32,12,128]{3,0,2,1:T(8,128)(2,1)} %bitcast.184, bf16[32,12,128,128]{3,2,1,0:T(8,128)(2,1)} %param.10), kind=kOutput, calls=%fused_computation.32 | convolution fusion | flops 805306368 | bytes 19922944 | tf_op jit(solution)/shard_map/kbpc,bpcr->kbr/dot_general | solution.py:42
  86.3 4.5 %all-to-all-done.1 = bf16[64,32,4,128]{3,0,2,1:T(8,128)(2,1)} async-done(((bf16[64,32,4,128]{3,0,2,1:T(8,128)(2,1)}), bf16[64,32,4,128]{3,0,2,1:T(8,128)(2,1)}, u32[]{:S(2)}, u32[]{:S(2)}) %all-to-all-start.1) | async-done | bytes 2097184 | tf_op jit(solution)/shard_map/all_to_all | solution.py:31
  90.8 2.5 gather_fusion.2
  93.4 3.1 fusion.5
  96.5 1.0 copy-done.5
  97.5 0.9 fusion.21
  98.4 28.6 %all-gather.7.cloned.1.call-done = bf16[64,128,128]{2,0,1:T(8,128)(2,1)} async-done(((bf16[64,32,128]{2,0,1:T(8,128)(2,1)}), bf16[64,128,128]{2,0,1:T(8,128)(2,1)}) %all-gather.7.cloned.1.call-update) | async-done | bytes 2097168 | tf_op jit(solution)/shard_map/all_gather | solution.py:40
  127.0 3.8 gather_fusion.4
  130.8 7.9 %all-to-all-start.2 = ((bf16[64,32,4,128]{3,0,2,1:T(8,128)(2,1)}), bf16[64,32,4,128]{3,0,2,1:T(8,128)(2,1)}, u32[]{:S(2)}, u32[]{:S(2)}) async-start(bf16[64,32,4,128]{3,0,2,1:T(8,128)(2,1)} %bitcast.190), calls=%async_computation.2 | async-start | bytes 4194304 | tf_op jit(solution)/shard_map/all_to_all | solution.py:31
  138.7 0.2 all-gather.9.cloned.1.call-start
  138.9 13.3 %gather_fusion.3 = bf16[384,64,128]{2,1,0:T(8,128)(2,1)} fusion(bf16[64,128,128]{2,0,1:T(8,128)(2,1)S(1)} %copy-done.3, s32[1024]{0:T(1024)S(1)} %pad_clamp_fusion.2), kind=kCustom, calls=%fused_computation.3 | custom fusion | bytes 12584448 | tf_op jit(solution)/shard_map/gather | solution.py:43
  152.2 9.0 %convolution_bitcast_fusion.6 = f32[32,64,128]{2,1,0:T(8,128)S(1)} fusion(bf16[64,32,12,128]{3,0,2,1:T(8,128)(2,1)} %bitcast.185, bf16[32,12,128,128]{3,2,1,0:T(8,128)(2,1)} %param.10), kind=kOutput, calls=%fused_computation.31 | convolution fusion | flops 805306368 | bytes 19922944 | tf_op jit(solution)/shard_map/kbpc,bpcr->kbr/dot_general | solution.py:42
  161.3 5.3 %all-to-all-done.2 = bf16[64,32,4,128]{3,0,2,1:T(8,128)(2,1)} async-done(((bf16[64,32,4,128]{3,0,2,1:T(8,128)(2,1)}), bf16[64,32,4,128]{3,0,2,1:T(8,128)(2,1)}, u32[]{:S(2)}, u32[]{:S(2)}) %all-to-all-start.2) | async-done | bytes 2097184 | tf_op jit(solution)/shard_map/all_to_all | solution.py:31
  166.6 2.5 gather_fusion.5
  169.1 3.2 fusion.3
  172.3 1.0 copy_bitcast_fusion
  173.4 28.6 %all-gather.9.cloned.1.call-done = bf16[64,128,128]{2,0,1:T(8,128)(2,1)} async-done(((bf16[64,32,128]{2,0,1:T(8,128)(2,1)}), bf16[64,128,128]{2,0,1:T(8,128)(2,1)}) %all-gather.9.cloned.1.call-update) | async-done | bytes 2097168 | tf_op jit(solution)/shard_map/all_gather | solution.py:40
  202.0 3.8 gather_fusion.7
  205.8 7.9 %all-to-all-start.3 = ((bf16[64,32,4,128]{3,0,2,1:T(8,128)(2,1)}), bf16[64,32,4,128]{3,0,2,1:T(8,128)(2,1)}, u32[]{:S(2)}, u32[]{:S(2)}) async-start(bf16[64,32,4,128]{3,0,2,1:T(8,128)(2,1)} %bitcast.191), calls=%async_computation.3 | async-start | bytes 4194304 | tf_op jit(solution)/shard_map/all_to_all | solution.py:31
  213.6 0.3 all-gather.11.cloned.1.call-start
  213.9 13.3 %gather_fusion.6 = bf16[384,64,128]{2,1,0:T(8,128)(2,1)} fusion(bf16[64,128,128]{2,0,1:T(8,128)(2,1)S(1)} %copy-done.4, s32[1024]{0:T(1024)S(1)} %pad_clamp_fusion.2), kind=kCustom, calls=%fused_computation.6 | custom fusion | bytes 12584448 | tf_op jit(solution)/shard_map/gather | solution.py:43
  227.2 9.0 %convolution_bitcast_fusion.5 = f32[32,64,128]{2,1,0:T(8,128)S(1)} fusion(bf16[64,32,12,128]{3,0,2,1:T(8,128)(2,1)} %bitcast.186, bf16[32,12,128,128]{3,2,1,0:T(8,128)(2,1)} %param.10), kind=kOutput, calls=%fused_computation.30 | convolution fusion | flops 805306368 | bytes 19922944 | tf_op jit(solution)/shard_map/kbpc,bpcr->kbr/dot_general | solution.py:42
  236.3 5.2 %all-to-all-done.3 = bf16[64,32,4,128]{3,0,2,1:T(8,128)(2,1)} async-done(((bf16[64,32,4,128]{3,0,2,1:T(8,128)(2,1)}), bf16[64,32,4,128]{3,0,2,1:T(8,128)(2,1)}, u32[]{:S(2)}, u32[]{:S(2)}) %all-to-all-start.3) | async-done | bytes 2097184 | tf_op jit(solution)/shard_map/all_to_all | solution.py:31
  241.5 3.8 gather_fusion.8
  245.3 4.6 %fusion.20 = (bf16[64,32,128]{2,0,1:T(8,128)(2,1)}, f32[32,64,128]{2,1,0:T(8,128)S(1)}) fusion(f32[32,128]{1,0:T(8,128)S(1)} %get-tuple-element.14, f32[32,64,128]{2,1,0:T(8,128)S(1)} %copy-done.6, f32[32,128]{1,0:T(8,128)S(1)} %broadcast_multiply_fusion.2, f32[32,64,128]{2,1,0:T(8,128)S(1)} %convolution_bitcast_fusion.5, ...), kind=kOutput, calls=%fused_computation.50 | convolution fusion | flops 270008320 | bytes 9994240 | tf_op jit(solution)/shard_map/kbpc,bpcr->kbr/dot_general | solution.py:45
  250.0 28.6 %all-gather.11.cloned.1.call-done = bf16[64,128,128]{2,0,1:T(8,128)(2,1)} async-done(((bf16[64,32,128]{2,0,1:T(8,128)(2,1)}), bf16[64,128,128]{2,0,1:T(8,128)(2,1)}) %all-gather.11.cloned.1.call-update) | async-done | bytes 2097168 | tf_op jit(solution)/shard_map/all_gather | solution.py:40
  278.5 3.8 gather_fusion.10
  282.3 8.3 %all-to-all-start.4 = ((bf16[64,32,4,128]{3,0,2,1:T(8,128)(2,1)}), bf16[64,32,4,128]{3,0,2,1:T(8,128)(2,1)}, u32[]{:S(2)}, u32[]{:S(2)}) async-start(bf16[64,32,4,128]{3,0,2,1:T(8,128)(2,1)} %bitcast.189), calls=%async_computation.4 | async-start | bytes 4194304 | tf_op jit(solution)/shard_map/all_to_all | solution.py:31
  290.6 1.0 convolution_bitcast_fusion.11
  291.6 13.3 %gather_fusion.9 = bf16[384,64,128]{2,1,0:T(8,128)(2,1)} fusion(bf16[64,128,128]{2,0,1:T(8,128)(2,1)S(1)} %copy-done.2, s32[1024]{0:T(1024)S(1)} %pad_clamp_fusion.2), kind=kCustom, calls=%fused_computation.9 | custom fusion | bytes 12584448 | tf_op jit(solution)/shard_map/gather | solution.py:43
  304.9 9.9 %convolution_bitcast_fusion.4 = f32[32,64,128]{2,1,0:T(8,128)} fusion(bf16[64,32,12,128]{3,0,2,1:T(8,128)(2,1)} %bitcast.183, bf16[32,12,128,128]{3,2,1,0:T(8,128)(2,1)} %param.10), kind=kOutput, calls=%fused_computation.29 | convolution fusion | flops 805306368 | bytes 19922944 | tf_op jit(solution)/shard_map/kbpc,bpcr->kbr/dot_general | solution.py:42
  314.9 3.5 all-to-all-done.4
  318.4 2.5 gather_fusion.11
  320.9 3.4 fusion.10
  324.3 1.0 convolution_bitcast_fusion.10
  325.3 64.7 %all-reduce = (f32[64,64]{0,1:T(8,128)S(1)}, f32[64,64]{0,1:T(8,128)S(1)}) all-reduce(f32[64,64]{0,1:T(8,128)S(1)} %convolution_bitcast_fusion.11, f32[64,64]{0,1:T(8,128)S(1)} %convolution_bitcast_fusion.10), channel_id=1, replica_groups=mesh['dom'=32,'sub'=4] {'dom','sub'}, use_global_device_ids=true, to_apply=%region_2.0 | all-reduce | flops 8192 | bytes 65536 | tf_op jit(solution)/shard_map/psum | solution.py:58
  390.2 5.8 %cholesky.16 = f32[64,64]{1,0:T(8,128)S(1)} custom-call(f32[64,64]{1,0:T(8,128)S(1)} %fusion.28), custom_call_target="Cholesky" | custom-call | tf_op jit(solution)/shard_map/jit(cholesky)/cholesky | solution.py:61
  396.0 0.6 compare_reduce_fusion
  396.7 0.7 fusion.24
  397.3 4.9 %custom-call.10 = f32[1,64,64]{1,2,0:T(8,128)S(1)} custom-call(f32[1,64,64]{2,1,0:T(8,128)S(1)} %fusion.24), custom_call_target="InvertDiagBlocksLowerTriangular" | custom-call | tf_op jit(solution)/shard_map/jit(_solve_triangular)/triangular_solve | solution.py:62
  402.2 2.0 fusion.14
  404.3 0.2 convolution_bitcast_fusion.9
  404.5 0.2 convolution_bitcast_fusion.8
  404.7 0.7 copy.47
  (41 shorter events, 0.4 us)
Async XLA Ops:
  7.2 44.1 %all-gather.5.cloned.1.call-start = ((), (), s32[]{:S(2)}) async-start(), calls=%async_computation.5 | async-start | bytes 2621440 | tf_op jit(solution)/shard_map/all_gather | solution.py:40
  7.2 7.8 %copy-start = (bf16[32,4,128,128]{3,2,1,0:T(8,128)(2,1)S(1)}, bf16[32,4,128,128]{3,2,1,0:T(8,128)(2,1)}, u32[]{:S(2)}) copy-start(bf16[32,4,128,128]{3,2,1,0:T(8,128)(2,1)} %param.11) | copy-start | bytes 12582916
  15.0 1.0 copy-start.7
  15.0 2.0 copy-start.11
  15.1 12.1 %copy-start.10 = (s32[1,1,4]{2,1,0:T(1,128)S(1)}, s32[1,1,4]{2,1,0:T(1,128)}, u32[]{:S(2)}) copy-start(s32[1,1,4]{2,1,0:T(1,128)} %param.14) | copy-start | bytes 52
  17.7 16.3 %all-to-all-start = ((s32[32,1,4]{2,1,0:T(1,128)}), s32[32,1,4]{2,1,0:T(1,128)S(1)}, u32[]{:S(2)}, u32[]{:S(2)}) async-start(s32[32,1,4]{2,1,0:T(1,128)} %copy.37), calls=%async_computation | async-start | bytes 32768 | tf_op jit(solution)/shard_map/all_to_all | solution.py:27
  55.1 8.4 %copy-start.9 = (s32[32,12]{0,1:T(8,128)S(1)}, s32[32,12]{0,1:T(8,128)}, u32[]{:S(2)}) copy-start(s32[32,12]{0,1:T(8,128)} %param.12) | copy-start | bytes 4612
  55.1 8.7 %copy-start.12 = (s32[32,4]{0,1:T(4,128)S(1)}, s32[32,4]{0,1:T(4,128)}, u32[]{:S(2)}) copy-start(s32[32,4]{0,1:T(4,128)} %param.13) | copy-start | bytes 1540
  55.1 8.9 %copy-start.1 = (bf16[64,128,128]{2,0,1:T(8,128)(2,1)S(1)}, bf16[64,128,128]{2,0,1:T(8,128)(2,1)}, u32[]{:S(2)}) copy-start(bf16[64,128,128]{2,0,1:T(8,128)(2,1)} %all-gather.5.cloned.1.call-done) | copy-start | bytes 6291460
  55.1 35.8 %all-to-all-start.1 = ((bf16[64,32,4,128]{3,0,2,1:T(8,128)(2,1)}), bf16[64,32,4,128]{3,0,2,1:T(8,128)(2,1)}, u32[]{:S(2)}, u32[]{:S(2)}) async-start(bf16[64,32,4,128]{3,0,2,1:T(8,128)(2,1)} %bitcast.188), calls=%async_computation.1 | async-start | bytes 4194304 | tf_op jit(solution)/shard_map/all_to_all | solution.py:31
  62.9 64.1 %all-gather.7.cloned.1.call-start = ((), (), s32[]{:S(2)}) async-start(), calls=%async_computation.6 | async-start | bytes 2621440 | tf_op jit(solution)/shard_map/all_gather | solution.py:40
  96.5 1.0 copy-start.5
  130.8 8.1 %copy-start.3 = (bf16[64,128,128]{2,0,1:T(8,128)(2,1)S(1)}, bf16[64,128,128]{2,0,1:T(8,128)(2,1)}, u32[]{:S(2)}) copy-start(bf16[64,128,128]{2,0,1:T(8,128)(2,1)} %all-gather.7.cloned.1.call-done) | copy-start | bytes 6291460
  130.8 35.8 %all-to-all-start.2 = ((bf16[64,32,4,128]{3,0,2,1:T(8,128)(2,1)}), bf16[64,32,4,128]{3,0,2,1:T(8,128)(2,1)}, u32[]{:S(2)}, u32[]{:S(2)}) async-start(bf16[64,32,4,128]{3,0,2,1:T(8,128)(2,1)} %bitcast.190), calls=%async_computation.2 | async-start | bytes 4194304 | tf_op jit(solution)/shard_map/all_to_all | solution.py:31
  138.7 63.3 %all-gather.9.cloned.1.call-start = ((), (), s32[]{:S(2)}) async-start(), calls=%async_computation.7 | async-start | bytes 2621440 | tf_op jit(solution)/shard_map/all_gather | solution.py:40
  169.1 3.2 copy-start.8
  205.8 8.1 %copy-start.4 = (bf16[64,128,128]{2,0,1:T(8,128)(2,1)S(1)}, bf16[64,128,128]{2,0,1:T(8,128)(2,1)}, u32[]{:S(2)}) copy-start(bf16[64,128,128]{2,0,1:T(8,128)(2,1)} %all-gather.9.cloned.1.call-done) | copy-start | bytes 6291460
  205.8 35.8 %all-to-all-start.3 = ((bf16[64,32,4,128]{3,0,2,1:T(8,128)(2,1)}), bf16[64,32,4,128]{3,0,2,1:T(8,128)(2,1)}, u32[]{:S(2)}, u32[]{:S(2)}) async-start(bf16[64,32,4,128]{3,0,2,1:T(8,128)(2,1)} %bitcast.191), calls=%async_computation.3 | async-start | bytes 4194304 | tf_op jit(solution)/shard_map/all_to_all | solution.py:31
  213.6 64.9 %all-gather.11.cloned.1.call-start = ((), (), s32[]{:S(2)}) async-start(), calls=%async_computation.8 | async-start | bytes 2621440 | tf_op jit(solution)/shard_map/all_gather | solution.py:40
  241.5 3.8 copy-start.6
  282.3 9.3 %copy-start.2 = (bf16[64,128,128]{2,0,1:T(8,128)(2,1)S(1)}, bf16[64,128,128]{2,0,1:T(8,128)(2,1)}, u32[]{:S(2)}) copy-start(bf16[64,128,128]{2,0,1:T(8,128)(2,1)} %all-gather.11.cloned.1.call-done) | copy-start | bytes 6291460
  282.3 36.0 %all-to-all-start.4 = ((bf16[64,32,4,128]{3,0,2,1:T(8,128)(2,1)}), bf16[64,32,4,128]{3,0,2,1:T(8,128)(2,1)}, u32[]{:S(2)}, u32[]{:S(2)}) async-start(bf16[64,32,4,128]{3,0,2,1:T(8,128)(2,1)} %bitcast.189), calls=%async_computation.4 | async-start | bytes 4194304 | tf_op jit(solution)/shard_map/all_to_all | solution.py:31
Sparse Core Ops, SparseCore 0:
  17.2 34.0 all-gather.4
  98.6 28.4 all-gather.6
  173.5 28.4 all-gather.8
  250.1 28.3 all-gather.10
where the time goes:
time: 418 us; the launch traced here: 412 us
  waiting for transfers between devices  125 us (30%)
  local copies, waits for them, and re-layouts  83.9 us (20%)
  blocking collectives  64.7 us (15%)
  matrix products  55.8 us (13%)
  starting transfers between devices  42.4 us (10%)
  other arithmetic  26.3 us (6%)
  between operations  14.7 us (4%)
    all_gather x4, waiting for transfers between devices, operate(): partition = lax.all_gather(scaled, 'sub', axis=1, tiled=True)  100 us
    psum x1, blocking collectives, body(): lax.psum((gram_local, rayleigh_local), ('dom', 'sub'))  64.7 us
    gather x4, local copies, waits for them, and re-layouts, operate(): partition[:, in_cols]  53.3 us
    dot_general x4, matrix products, operate(): jnp.einsum('kbpc,bpcr->kbr', partition[:, in_cols], tiles_in, preferred_e...  37 us
    all_to_all x4, starting transfers between devices, fetch(): lax.all_to_all(outgoing, 'dom', split_axis=1, concat_axis=1, tiled=True)  31.9 us
    all_to_all x4, waiting for transfers between devices, fetch(): lax.all_to_all(outgoing, 'dom', split_axis=1, concat_axis=1, tiled=True)  18.5 us
    gather x4, local copies, waits for them, and re-layouts, fetch(): outgoing = partition[:, wanted, :]  15.2 us
    dot_general x4, matrix products, operate(): jnp.einsum('kbpc,bpcr->kbr', remote[:, out_cols], tiles_out, preferred_el...  14.3 us
  transfers between devices with their start and end apart: 9, of which 9 were waited for; matrix products, arithmetic and copies ran while one was open for 23% of the time, Pallas kernels for 0%

commit v1 on v0

v1 whole, which is shorter than its diff:
```python
import functools
import math

import jax
import jax.numpy as jnp
from jax import lax
from jax.experimental import pallas as pl
from jax.experimental.pallas import tpu as pltpu
from jax.sharding import PartitionSpec as P

MESH = pl.DeviceIdType.MESH
HIGHEST = lax.Precision.HIGHEST
F32 = jnp.float32
BF16 = jnp.bfloat16
OPS = 4
NC = 4


def nt(a, b):
    return lax.dot_general(
        a, b, (((1,), (1,)), ((), ())), precision=HIGHEST, preferred_element_type=F32
    )


def kernel(
    rows_total, spectral, count,
    start_ref, tin_hbm, tout_hbm, ic, oc, exp_ref, recv_ref,
    basis_ref, proj_ref,
    tin, tout, *scratch,
):
    parts = [scratch[NC * p : NC * p + NC] for p in range(2)]
    scratch = scratch[2 * NC :]
    outs = [scratch[NC * p : NC * p + NC] for p in range(2)]
    (vec, acc, dinv, rowf, oidx, mat, gram_bufs, ray_bufs,
     load_sem, y_send, y_recv, xz_send, xz_recv, core_send, core_recv,
     ar_send, ar_recv) = scratch[2 * NC :]
    width = start_ref.shape[0]
    kc = width // NC
    nb, tp_in = tin.shape[:2]
    tp_out = tout.shape[1]
    tile = tin.shape[2]
    half = nb // 2
    offered = exp_ref.shape[0]

    dom = lax.axis_index("dom")
    s = lax.axis_index("sub")
    z, x, core = dom // 8, (dom // 2) % 4, dom % 2

    def dev(dz, dx, dy, dc):
        zz, xx, cc = (z + dz) % 4, (x + dx) % 4, (core + dc) % 2
        return (zz * 8 + xx * 2 + cc, (s + dy) % 4)

    plane = [(dz, dx) for dz in range(4) for dx in range(4) if (dz, dx) != (0, 0)]
    right, left, partner = dev(0, 0, 1, 0), dev(0, 0, 3, 0), dev(0, 0, 0, 1)

    barrier = pltpu.get_barrier_semaphore()
    friends = [dev(dz, dx, 0, 0) for dz, dx in plane]
    friends += [dev(0, 0, dy, 0) for dy in (1, 2, 3)] + [partner]
    for f in friends:
        pl.semaphore_signal(barrier, inc=1, device_id=f, device_id_type=MESH)

    pieces = load_sem.shape[0]
    step = nb // pieces
    loads = []
    for i in range(pieces):
        rows = pl.ds(i * step, step)
        a = pltpu.make_async_copy(tin_hbm.at[rows], tin.at[rows], load_sem.at[i, 0])
        b = pltpu.make_async_copy(tout_hbm.at[rows], tout.at[rows], load_sem.at[i, 1])
        a.start()
        b.start()
        loads.append((a, b))

    def slot_of(i, carry):
        b, t = i // tp_out, i % tp_out
        v = oc[b, t]
        g = v // offered
        oidx[b, t] = (g % 2) * (16 * offered) + (g // 2) * offered + recv_ref[v]
        return carry

    lax.fori_loop(0, nb * tp_out, slot_of, 0)
    for b in range(nb):
        vec[0, b] = start_ref[:, b * tile : (b + 1) * tile].astype(F32)

    def total(ref, b, n):
        a = jnp.abs(ref[b].reshape(n * tile, tile)).astype(F32)
        return jnp.sum(a.reshape(n * tile // 8, 8, tile), axis=0)

    for i in range(pieces):
        for cp in loads[i]:
            cp.wait()

        def degree(b, carry):
            mag = jnp.sum(total(tin, b, tp_in) + total(tout, b, tp_out), axis=0, keepdims=True)
            inv = 1.0 / jnp.sqrt(mag / count + 1e-06)
            dinv[b] = jnp.broadcast_to(inv, (8, tile))
            rowf[b] = jnp.broadcast_to(spectral * inv, (8, tile))
            return carry

        lax.fori_loop(i * step, (i + 1) * step, degree, 0, unroll=2)

    pl.semaphore_wait(barrier, len(friends))

    own = s * nb
    base = core * (16 * offered) + (z * 4 + x) * offered

    def y_copies(j):
        part = parts[(j // NC) % 2][j % NC]

        def cp(k, first, to):
            block = part.at[pl.ds(first, half)]
            return pltpu.make_async_remote_copy(
                src_ref=block, dst_ref=block, send_sem=y_send.at[j, k],
                recv_sem=y_recv.at[j, k], device_id=to, device_id_type=MESH,
            )

        lo = ((s + 3) % 4) * nb
        hi = ((s + 1) % 4) * nb
        sends = [cp(0, own, right), cp(1, own + half, left), cp(2, own + half, right), cp(3, own, left)]
        forwards = [cp(4, lo, right), cp(5, hi + half, left)]
        return sends, forwards

    def send_own(j):
        for cp in y_copies(j)[0]:
            cp.start()

    def forward(j):
        sends, forwards = y_copies(j)
        for k in range(2):
            sends[k].wait_recv()
            forwards[k].start()

    def xz_copies(j):
        out = outs[(j // NC) % 2][j % NC]
        block = out.at[pl.ds(base, offered)]
        return [
            pltpu.make_async_remote_copy(
                src_ref=block, dst_ref=block, send_sem=xz_send.at[j], recv_sem=xz_recv.at[j],
                device_id=dev(dz, dx, 0, 0), device_id_type=MESH,
            )
            for dz, dx in plane
        ]

    def wait_bytes(out, sem):
        view = out.at[pl.ds(0, len(plane) * offered)]
        pltpu.make_async_copy(view, view, sem).wait()

    def export(j):
        sends, forwards = y_copies(j)
        sends[2].wait_recv()
        sends[3].wait_recv()
        for cp in forwards:
            cp.wait_recv()
        for cp in sends:
            cp.wait_send()
        part = parts[(j // NC) % 2][j % NC]
        out = outs[(j // NC) % 2][j % NC]
        for e in range(offered):
            out[base + e] = part[exp_ref[e]]
        for cp in xz_copies(j):
            cp.start()

    def core_copy(j):
        block = outs[(j // NC) % 2][j % NC].at[pl.ds(core * (16 * offered), 16 * offered)]
        return pltpu.make_async_remote_copy(
            src_ref=block, dst_ref=block, send_sem=core_send.at[j], recv_sem=core_recv.at[j],
            device_id=partner, device_id_type=MESH,
        )

    def share(j):
        out = outs[(j // NC) % 2][j % NC]
        wait_bytes(out, xz_recv.at[j])
        core_copy(j).start()
        wait_bytes(out, xz_send.at[j])
        for cp in y_copies(j)[1]:
            cp.wait_send()

    def inner(j, first, last):
        part, c = parts[(j // NC) % 2][j % NC], j % NC

        def one(b, carry):
            v = jnp.concatenate([part[ic[b, t]] for t in range(tp_in)], axis=1)
            acc[c, b] = jnp.dot(v, tin[b].reshape(tp_in * tile, tile), preferred_element_type=F32)
            return carry

        lax.fori_loop(first, last, one, 0, unroll=4)

    def scale(part, c, b, new):
        part[own + b] = (new * dinv[b, :1, :]).astype(BF16)

    def outer(j):
        n, c = j // NC, j % NC
        core_copy(j).wait_recv()
        core_copy(j).wait_send()
        out = outs[n % 2][c]
        rows = pl.ds(c * kc, kc)
        p = (n + 1) % 2

        def one(b, carry):
            v = jnp.concatenate([out[oidx[b, t]] for t in range(tp_out)], axis=1)
            o = acc[c, b] + jnp.dot(v, tout[b].reshape(tp_out * tile, tile), preferred_element_type=F32)
            new = o * rowf[b, :1, :]
            if n in (1, 2):
                new = 2.0 * new - vec[p, b, rows, :]
            vec[p, b, rows, :] = new
            if n + 1 < OPS:
                scale(parts[p][c], c, b, new)
            return carry

        lax.fori_loop(0, nb, one, 0, unroll=4)

    axes = [
        (core, [dev(0, 0, 0, 1)]),
        (s, [dev(0, 0, d, 0) for d in (1, 2, 3)]),
        (x, [dev(0, d, 0, 0) for d in (1, 2, 3)]),
        (z, [dev(d, 0, 0, 0) for d in (1, 2, 3)]),
    ]

    def sum_copies(use, a):
        bufs = (gram_bufs, ray_bufs)[use]
        place, peers = axes[a]
        block = bufs.at[a, place]
        return [
            pltpu.make_async_remote_copy(
                src_ref=block, dst_ref=block, send_sem=ar_send.at[use, a], recv_sem=ar_recv.at[use, a],
                device_id=to, device_id_type=MESH,
            )
            for to in peers
        ]

    def sum_start(use, a, value):
        bufs = (gram_bufs, ray_bufs)[use]
        bufs[a, axes[a][0]] = value
        for cp in sum_copies(use, a):
            cp.start()

    def sum_end(use, a):
        bufs = (gram_bufs, ray_bufs)[use]
        n = len(axes[a][1])
        view = bufs.at[a, pl.ds(0, n)]
        pltpu.make_async_copy(view, view, ar_recv.at[use, a]).wait()
        pltpu.make_async_copy(view, view, ar_send.at[use, a]).wait()
        value = bufs[a, 0] + bufs[a, 1]
        for k in range(2, n + 1):
            value = value + bufs[a, k]
        return value

    fslot = OPS % 2 ^ 1
    group = 4

    def wide(slot, i, rows):
        return jnp.concatenate([vec[slot, i * group + k, rows, :] for k in range(group)], axis=1)

    def product(slot):
        def one(i, carry):
            return carry + nt(wide(slot, i, slice(None)), wide(fslot, i, slice(None)))

        zero = jnp.zeros((width, width), F32)
        got = lax.fori_loop(0, nb // group, one, zero)
        return jnp.concatenate([got, zero], axis=1)

    lane = lax.broadcasted_iota(jnp.int32, (1, 2 * width), 1)
    line = lax.broadcasted_iota(jnp.int32, (width, 1), 0)

    def eliminate(first, last):
        def one(k, carry):
            m = mat[...]
            row = mat[pl.ds(k, 1), :]
            inv = 1.0 / jnp.sqrt(jnp.sum(jnp.where(lane == k, row, 0.0), axis=1, keepdims=True))
            row = row * inv
            col = jnp.sum(jnp.where(lane == k, m, 0.0), axis=1, keepdims=True) * inv
            mat[...] = jnp.where(line > k, m - col * row, jnp.where(line == k, row, m))
            return carry

        lax.fori_loop(first, last, one, 0)

    def start_elimination(gram):
        eye = jnp.where(lane - width == line, 1.0, 0.0)
        mat[...] = jnp.where(lane < width, gram / rows_total, eye)

    for c in range(NC):
        def one(b, carry, c=c):
            scale(parts[0][c], c, b, vec[0, b, c * kc : (c + 1) * kc, :])
            return carry

        lax.fori_loop(0, nb, one, 0, unroll=4)
        send_own(c)

    stages = OPS * NC

    def has(j):
        return 0 <= j < stages

    for i in range(1, stages + NC):
        if i >= NC and has(i - 4):
            outer(i - 4)
        if i >= NC and has(i):
            send_own(i)
        if has(i - 1):
            forward(i - 1)
        if i == stages:
            sum_start(0, 0, product(fslot))
        if has(i - 2):
            export(i - 2)
            inner(i - 2, 0, nb // 2)
        if i == stages:
            sum_start(0, 1, sum_end(0, 0))
        if i == stages + 1:
            sum_start(0, 3, sum_end(0, 2))
        if has(i - 3):
            share(i - 3)
        if has(i - 2):
            inner(i - 2, nb // 2, nb)
        if i == stages:
            sum_start(0, 2, sum_end(0, 1))
        if i == stages + 1:
            start_elimination(sum_end(0, 3))
        if i == stages + 2:
            eliminate(0, width)

    sum_start(1, 0, product(1 - fslot))
    linv = mat[...][:, width:]
    for a in range(4):
        for i in range(a * 2, a * 2 + 2):
            got = jnp.dot(linv, wide(fslot, i, slice(None)), precision=HIGHEST, preferred_element_type=F32)
            basis_ref[:, i * group * tile : (i + 1) * group * tile] = got
        value = sum_end(1, a)
        if a < 3:
            sum_start(1, a + 1, value)
    rayleigh_t = value[:, :width] / rows_total
    proj_ref[...] = nt(nt(linv, rayleigh_t), linv)


def body(start_block, tiles_in, tiles_out, in_cols, out_cols, export_list, recv_list):
    width, local_rows = start_block.shape
    nb, tp_in, tile, _ = tiles_in.shape
    tp_out = tiles_out.shape[1]
    count = (tp_in + tp_out) * tile
    devices = lax.axis_size("dom") * lax.axis_size("sub")
    kc = width // NC
    stages = OPS * NC
    blocks = nb * 4
    slots = recv_list.size
    smem = pl.BlockSpec(memory_space=pltpu.SMEM)
    hbm = pl.BlockSpec(memory_space=pl.ANY)
    vmem = pl.BlockSpec(memory_space=pltpu.VMEM)
    dma = pltpu.SemaphoreType.DMA
    return pl.pallas_call(
        functools.partial(
            kernel, local_rows * devices, 1.0 / (1.25 * math.sqrt(count)), count
        ),
        out_shape=(
            jax.ShapeDtypeStruct((width, local_rows), F32),
            jax.ShapeDtypeStruct((width, width), F32),
        ),
        in_specs=[vmem, hbm, hbm, smem, smem, smem, smem],
        out_specs=(vmem, vmem),
        scratch_shapes=[
            pltpu.VMEM(tiles_in.shape, BF16),
            pltpu.VMEM(tiles_out.shape, BF16),
            *[pltpu.VMEM((blocks, kc, tile), BF16) for _ in range(2 * NC)],
            *[pltpu.VMEM((slots, kc, tile), BF16) for _ in range(2 * NC)],
            pltpu.VMEM((2, nb, width, tile), F32),
            pltpu.VMEM((NC, nb, kc, tile), F32),
            pltpu.VMEM((nb, 8, tile), F32),
            pltpu.VMEM((nb, 8, tile), F32),
            pltpu.SMEM((nb, tp_out), jnp.int32),
            pltpu.VMEM((width, 2 * width), F32),
            pltpu.VMEM((4, 4, width, 2 * width), F32),
            pltpu.VMEM((4, 4, width, 2 * width), F32),
            dma((8, 2)),
            dma((stages, 6)),
            dma((stages, 6)),
            dma((stages,)),
            dma((stages,)),
            dma((stages,)),
            dma((stages,)),
            dma((2, 4)),
            dma((2, 4)),
        ],
        compiler_params=pltpu.CompilerParams(
            collective_id=0, has_side_effects=True, vmem_limit_bytes=48 << 20
        ),
        name="filtered_step",
    )(
        start_block, tiles_in, tiles_out, in_cols, out_cols,
        export_list.reshape(-1), recv_list.reshape(-1),
    )


def solution(mesh):
    return jax.shard_map(
        body,
        mesh=mesh,
        in_specs=(
            P(None, ("dom", "sub")),
            P(("dom", "sub"), None, None, None),
            P(("dom", "sub"), None, None, None),
            P(("dom", "sub"), None),
            P(("dom", "sub"), None),
            P("dom", "sub", None),
            P("dom", "sub", None, None),
        ),
        out_specs=(P(None, ("dom", "sub")), P()),
        check_vma=False,
    )
```

time: 418 us -> 159 us (0.38); the launches traced: 412 us -> 158 us
  Pallas kernels: 0 us -> 150 us
  waiting for transfers between devices: 125 us -> 0 us
  local copies, waits for them, and re-layouts: 83.9 us -> 7.87 us
  blocking collectives: 64.7 us -> 0 us
  matrix products: 55.8 us -> 0 us
  starting transfers between devices: 42.4 us -> 0 us
  other arithmetic: 26.3 us -> 0 us
  between operations: 14.7 us -> 0.65 us
    pallas_call x0 -> x1, Pallas kernels: none -> 150 us  [body(): pl.pallas_call(functools.partial(kernel, local_rows * devices, 1.0 / (1.2...]
    all_gather x4 -> x0, waiting for transfers between devices: 100 us -> none  [operate(): partition = lax.all_gather(scaled, 'sub', axis=1, tiled=True)]
    gather x13 -> x0, local copies, waits for them, and re-layouts: 80.6 us -> none  [the longest x4 53.3 us: operate(): partition[:, in_cols]]
    psum x1 -> x0, blocking collectives: 64.7 us -> none  [body(): lax.psum((gram_local, rayleigh_local), ('dom', 'sub'))]
    dot_general x10 -> x0, matrix products: 53.3 us -> none  [the longest x4 37 us: operate(): jnp.einsum('kbpc,bpcr->kbr', partition[:, in_cols], tiles_in, preferred_e...]
    all_to_all x5 -> x0, starting transfers between devices: 41.3 us -> none  [the longest x4 31.9 us: fetch(): lax.all_to_all(outgoing, 'dom', split_axis=1, concat_axis=1, tiled=True)]
    all_to_all x5 -> x0, waiting for transfers between devices: 24.7 us -> none  [the longest x4 18.5 us: fetch(): lax.all_to_all(outgoing, 'dom', split_axis=1, concat_axis=1, tiled=True)]
    another operation x5 -> x0, other arithmetic: 12.1 us -> none  [the longest x3 6.52 us: body(): lower = jnp.linalg.cholesky(gram)]
  transfers between devices with their start and end apart: 9 -> 0, of which waited for: 9 -> 0; matrix products, arithmetic and copies ran while one was open for 23% -> 0% of each run, Pallas kernels for 0% -> 0%
where the time goes in v1:
time: 159 us; the launch traced here: 158 us
  Pallas kernels  150 us (94%)
  local copies, waits for them, and re-layouts  7.87 us (5%)
    pallas_call x1, Pallas kernels, body(): pl.pallas_call(functools.partial(kernel, local_rows * devices, 1.0 / (1.2...  150 us
    unnamed x11, local copies, waits for them, and re-layouts  7.77 us

profile of v1, /device:TPU:1, one launch (start us, length us, event | category | flops | bytes accessed | tf_op | source)
XLA Modules:
  0.0 158.0 jit_solution(556456528176149662)
XLA Ops:
  0.6 0.8 copy.13.ic
  1.4 0.8 copy.14.oc
  2.2 0.8 copy.12
  2.9 0.1 reshape.11.recv_ref
  3.0 0.0 copy-start
  3.0 2.2 %copy-done = bf16[32,4,128,128]{3,2,1,0:T(8,128)(2,1)S(1)} copy-done((bf16[32,4,128,128]{3,2,1,0:T(8,128)(2,1)S(1)}, bf16[32,4,128,128]{3,2,1,0:T(8,128)(2,1)}, u32[]{:S(2)}) %copy-start) | copy-done | bytes 4194328
  5.2 0.0 copy-start.1
  5.2 1.0 copy-done.1
  6.3 0.0 copy-start.2
  6.3 0.7 copy-done.2
  6.9 149.5 %filtered_step.1 = (f32[64,4096]{1,0:T(8,128)S(1)}, f32[64,64]{1,0:T(8,128)S(1)}) custom-call(bf16[64,4096]{1,0:T(8,128)(2,1)S(1)} %copy-done.1, bf16[32,12,128,128]{3,2,1,0:T(8,128)(2,1)} %tin_hbm.1, bf16[32,4,128,128]{3,2,1,0:T(8,128)(2,1)S(1)} %copy-done, s32[32,12]{1,0:T(8,128)S(1)} %copy.13.ic, s32[32,4]{1,0:T(8,128)S(1)} %copy.14.oc, s32[4]{0:T(128)S(1)} %bitcast.3, ...), custom_call_target="tpu_custom_call" | custom-call | tf_op jit(solution)/shard_map/filtered_step/pallas_call | solution.py:347
  156.4 1.0 copy.17
  157.4 0.6 copy.18
Async XLA Ops:
  3.0 2.2 %copy-start = (bf16[32,4,128,128]{3,2,1,0:T(8,128)(2,1)S(1)}, bf16[32,4,128,128]{3,2,1,0:T(8,128)(2,1)}, u32[]{:S(2)}) copy-start(bf16[32,4,128,128]{3,2,1,0:T(8,128)(2,1)} %tout_hbm.1) | copy-start | bytes 12582916
  5.2 1.0 copy-start.1
  6.3 0.7 copy-start.2

commit v2 on v1

v2 whole, which is shorter than its diff:
```python
import functools
import math

import jax
import jax.numpy as jnp
from jax import lax
from jax.experimental import pallas as pl
from jax.experimental.pallas import tpu as pltpu
from jax.sharding import PartitionSpec as P

MESH = pl.DeviceIdType.MESH
HIGHEST = lax.Precision.HIGHEST
F32 = jnp.float32
BF16 = jnp.bfloat16
OPS = 4
NC = 4


def nt(a, b):
    return lax.dot_general(
        a, b, (((1,), (1,)), ((), ())), precision=HIGHEST, preferred_element_type=F32
    )


def kernel(
    rows_total, spectral, count,
    start_hbm, tin_hbm, tout_hbm, ic_hbm, oc_hbm, exp_hbm, recv_hbm,
    basis_ref, proj_ref,
    start_ref, tin, tout, *scratch,
):
    raws = scratch[:NC]
    scratch = scratch[NC:]
    parts = [scratch[NC * p : NC * p + NC] for p in range(2)]
    scratch = scratch[2 * NC :]
    outs = [scratch[NC * p : NC * p + NC] for p in range(2)]
    (vec, acc, dinv, rowf, dall, ic, oc, exp_ref, recv_ref, oidx, mat, ray, near, far, basis_vmem,
     table_sem, start_sem, load_sem, d_send, d_recv, y_send, y_recv, xz_send, xz_recv, core_send, core_recv,
     sum_send, sum_recv, basis_sem) = scratch[2 * NC :]
    width = start_ref.shape[0]
    kc = width // NC
    nb, tp_in = tin.shape[:2]
    tp_out = tout.shape[1]
    tile = tin.shape[2]
    half = nb // 2
    offered = exp_hbm.shape[0]

    dom = lax.axis_index("dom")
    s = lax.axis_index("sub")
    z, x, core = dom // 8, (dom // 2) % 4, dom % 2

    def dev(dz, dx, dy, dc):
        zz, xx, cc = (z + dz) % 4, (x + dx) % 4, (core + dc) % 2
        return (zz * 8 + xx * 2 + cc, (s + dy) % 4)

    plane = [(dz, dx) for dz in range(4) for dx in range(4) if (dz, dx) != (0, 0)]
    right, left, partner = dev(0, 0, 1, 0), dev(0, 0, 3, 0), dev(0, 0, 0, 1)

    barrier = pltpu.get_barrier_semaphore()
    friends = [dev(dz, dx, 0, 0) for dz, dx in plane]
    friends += [dev(0, 0, dy, dc) for dy in range(4) for dc in range(2) if (dy, dc) != (0, 0)]
    for f in friends:
        pl.semaphore_signal(barrier, inc=1, device_id=f, device_id_type=MESH)

    start_copy = pltpu.make_async_copy(start_hbm, start_ref, start_sem)
    start_copy.start()
    pieces = load_sem.shape[0]
    step = nb // pieces
    loads = []
    for i in range(pieces):
        rows = pl.ds(i * step, step)
        a = pltpu.make_async_copy(tin_hbm.at[rows], tin.at[rows], load_sem.at[i, 0])
        b = pltpu.make_async_copy(tout_hbm.at[rows], tout.at[rows], load_sem.at[i, 1])
        a.start()
        b.start()
        loads.append((a, b))

    own = s * nb
    table_copies = [
        pltpu.make_async_copy(a, b, table_sem.at[i])
        for i, (a, b) in enumerate(((ic_hbm, ic), (oc_hbm, oc), (exp_hbm, exp_ref), (recv_hbm, recv_ref)))
    ]
    for cp in table_copies:
        cp.start()

    def slot_of(i, carry):
        b, t = i // tp_out, i % tp_out
        v = oc[t, b]
        g, e = v // offered, v % offered
        oidx[t, b] = (g % 2) * (16 * offered) + (g // 2) * offered + recv_ref[e, g]
        return carry

    def total(ref, b, n):
        a = jnp.abs(ref[b].reshape(n * tile, tile)).astype(F32)
        return jnp.sum(a.reshape(n * tile // 8, 8, tile), axis=0)

    def degrees(first, last):
        for i in range(first, last):
            for cp in loads[i]:
                cp.wait()

            def degree(b, carry):
                mag = jnp.sum(total(tin, b, tp_in) + total(tout, b, tp_out), axis=0, keepdims=True)
                inv = 1.0 / jnp.sqrt(mag / count + 1e-06)
                dall[pl.ds(own + b, 1), :] = inv
                dinv[b] = jnp.broadcast_to(inv, (8, tile))
                rowf[b] = jnp.broadcast_to(spectral * inv, (8, tile))
                return carry

            lax.fori_loop(i * step, (i + 1) * step, degree, 0, unroll=True)

    def degree_copies():
        block = dall.at[pl.ds(own, nb)]
        return [
            pltpu.make_async_remote_copy(
                src_ref=block, dst_ref=block, send_sem=d_send, recv_sem=d_recv,
                device_id=dev(0, 0, d, 0), device_id_type=MESH,
            )
            for d in (1, 2, 3)
        ]

    def degrees_end():
        view = dall.at[pl.ds(0, 3 * nb)]
        pltpu.make_async_copy(view, view, d_recv).wait()
        pltpu.make_async_copy(view, view, d_send).wait()

    base = core * (16 * offered) + (z * 4 + x) * offered

    def y_copies(j):
        part = raws[j] if j < NC else parts[(j // NC) % 2][j % NC]

        def cp(k, first, to):
            block = part.at[pl.ds(first, half)]
            return pltpu.make_async_remote_copy(
                src_ref=block, dst_ref=block, send_sem=y_send.at[j, k],
                recv_sem=y_recv.at[j, k], device_id=to, device_id_type=MESH,
            )

        lo = ((s + 3) % 4) * nb
        hi = ((s + 1) % 4) * nb
        sends = [cp(0, own, right), cp(1, own + half, left), cp(2, own + half, right), cp(3, own, left)]
        forwards = [cp(4, lo, right), cp(5, hi + half, left)]
        return sends, forwards

    def send_own(j, later=None):
        sends = y_copies(j)[0]
        sends[0].start()
        sends[1].start()
        if later is not None:
            forward(later)
        sends[2].start()
        sends[3].start()

    def forward(j):
        sends, forwards = y_copies(j)
        for k in range(2):
            sends[k].wait_recv()
            forwards[k].start()

    def xz_copies(j):
        out = outs[(j // NC) % 2][j % NC]
        block = out.at[pl.ds(base, offered)]
        return [
            pltpu.make_async_remote_copy(
                src_ref=block, dst_ref=block, send_sem=xz_send.at[j], recv_sem=xz_recv.at[j],
                device_id=dev(dz, dx, 0, 0), device_id_type=MESH,
            )
            for dz, dx in plane
        ]

    def wait_bytes(out, sem):
        view = out.at[pl.ds(0, len(plane) * offered)]
        pltpu.make_async_copy(view, view, sem).wait()

    def export(j):
        sends, forwards = y_copies(j)
        sends[2].wait_recv()
        sends[3].wait_recv()
        for cp in forwards:
            cp.wait_recv()
        for cp in sends:
            cp.wait_send()
        part = parts[(j // NC) % 2][j % NC]
        out = outs[(j // NC) % 2][j % NC]
        if j < NC:

            def one(k, carry):
                part[k] = (raws[j][k].astype(F32) * dall[pl.ds(k, 1), :]).astype(BF16)
                return carry

            lax.fori_loop(0, 4 * nb, one, 0, unroll=8)
        for e in range(offered):
            out[base + e] = part[exp_ref[e]]
        for cp in xz_copies(j):
            cp.start()

    def core_copy(j):
        block = outs[(j // NC) % 2][j % NC].at[pl.ds(core * (16 * offered), 16 * offered)]
        return pltpu.make_async_remote_copy(
            src_ref=block, dst_ref=block, send_sem=core_send.at[j], recv_sem=core_recv.at[j],
            device_id=partner, device_id_type=MESH,
        )

    def share(j):
        out = outs[(j // NC) % 2][j % NC]
        wait_bytes(out, xz_recv.at[j])
        core_copy(j).start()
        wait_bytes(out, xz_send.at[j])
        for cp in y_copies(j)[1]:
            cp.wait_send()

    def inner(j, first, last):
        part, c = parts[(j // NC) % 2][j % NC], j % NC

        def one(b, carry):
            v = jnp.concatenate([part[ic[t, b]] for t in range(tp_in)], axis=1)
            acc[c, b] = jnp.dot(v, tin[b].reshape(tp_in * tile, tile), preferred_element_type=F32)
            return carry

        lax.fori_loop(first, last, one, 0, unroll=8)

    def scale(part, c, b, new):
        part[own + b] = (new * dinv[b, :1, :]).astype(BF16)

    def outer(j):
        n, c = j // NC, j % NC
        core_copy(j).wait_recv()
        core_copy(j).wait_send()
        out = outs[n % 2][c]
        rows = pl.ds(c * kc, kc)
        p = (n + 1) % 2

        def one(b, carry):
            v = jnp.concatenate([out[oidx[t, b]] for t in range(tp_out)], axis=1)
            o = acc[c, b] + jnp.dot(v, tout[b].reshape(tp_out * tile, tile), preferred_element_type=F32)
            new = o * rowf[b, :1, :]
            if n in (1, 2):
                new = 2.0 * new - vec[p, b, rows, :]
            vec[p, b, rows, :] = new
            if n + 1 < OPS:
                scale(parts[p][c], c, b, new)
            return carry

        lax.fori_loop(0, nb, one, 0, unroll=8)

    fslot = OPS % 2 ^ 1
    group = 4

    def wide(slot, i, rows):
        return jnp.concatenate([vec[slot, i * group + k, rows, :] for k in range(group)], axis=1)

    def product(slot):
        def one(i, carry):
            return carry + nt(wide(slot, i, slice(None)), wide(fslot, i, slice(None)))

        zero = jnp.zeros((width, width), F32)
        return lax.fori_loop(0, nb // group, one, zero)

    def rayleigh(j):
        rows = pl.ds((j % NC) * kc, kc)

        def one(i, carry):
            return carry + nt(wide(1 - fslot, i, rows), wide(fslot, i, slice(None)))

        ray[rows, :] = lax.fori_loop(0, nb // group, one, jnp.zeros((kc, width), F32))

    def spread(use, k):
        buf = (near, far)[k].at[use]
        if k == 0:
            block = buf.at[core * 4 + s]
            peers = [dev(0, 0, dy, dc) for dy in range(4) for dc in range(2) if (dy, dc) != (0, 0)]
        else:
            block = buf.at[z * 4 + x]
            peers = [dev(dz, dx, 0, 0) for dz, dx in plane]
        return [
            pltpu.make_async_remote_copy(
                src_ref=block, dst_ref=block, send_sem=sum_send.at[use, k], recv_sem=sum_recv.at[use, k],
                device_id=to, device_id_type=MESH,
            )
            for to in peers
        ]

    def sum_start(use, k, value):
        if k == 0:
            near[use, core * 4 + s] = value
        else:
            far[use, z * 4 + x] = value
        for cp in spread(use, k):
            cp.start()

    def sum_end(use, k):
        n = (8, 16)[k]
        buf = (near, far)[k].at[use]
        view = buf.at[pl.ds(0, n - 1)]
        pltpu.make_async_copy(view, view, sum_recv.at[use, k]).wait()
        pltpu.make_async_copy(view, view, sum_send.at[use, k]).wait()
        values = [buf[i] for i in range(n)]
        while len(values) > 1:
            values = [a + b for a, b in zip(values[::2], values[1::2])]
        return values[0]

    low = width // 2

    def pack(square):
        return jnp.concatenate([square[:low], square[low:]], axis=1)

    def unpack(packed):
        return jnp.concatenate([packed[:, :width], packed[:, width:]], axis=0)

    lane = lax.broadcasted_iota(jnp.int32, (1, 2 * width), 1)
    line = lax.broadcasted_iota(jnp.int32, (width, 1), 0)

    def eliminate(first, last):
        def one(k, carry):
            m = mat[...]
            row = mat[pl.ds(k, 1), :]
            inv = 1.0 / jnp.sqrt(jnp.sum(jnp.where(lane == k, row, 0.0), axis=1, keepdims=True))
            row = row * inv
            col = jnp.sum(jnp.where(lane == k, m, 0.0), axis=1, keepdims=True) * inv
            mat[...] = jnp.where(line > k, m - col * row, jnp.where(line == k, row, m))
            return carry

        lax.fori_loop(first, last, one, 0)

    def start_elimination(gram):
        eye = jnp.where(lane - width == line, 1.0, 0.0)
        gram = unpack(gram) / rows_total
        mat[...] = jnp.where(lane < width, jnp.concatenate([gram, gram], axis=1), eye)

    stages = OPS * NC

    def has(j):
        return 0 <= j < stages

    start_copy.wait()
    for b in range(nb):
        for c in range(NC):
            raws[c][own + b] = start_ref[c * kc : (c + 1) * kc, b * tile : (b + 1) * tile]
    pl.semaphore_wait(barrier, len(friends))
    send_own(0)
    for cp in table_copies:
        cp.wait()
    degrees(0, 3)
    send_own(1, 0)
    degrees(3, 6)
    send_own(2, 1)
    degrees(6, pieces)
    for cp in degree_copies():
        cp.start()
    send_own(3, 2)
    degrees_end()
    for i in range(2, stages + NC):
        if has(i - 4):
            outer(i - 4)
        if i - 4 >= stages - NC:
            rayleigh(i - 4)
        if i >= NC and has(i):
            send_own(i, i - 1)
        if i == stages:
            forward(i - 1)
        if i == stages - 1:
            sum_start(0, 0, pack(product(fslot)))
        if has(i - 2):
            export(i - 2)
            if i == 2:
                lax.fori_loop(0, nb * tp_out, slot_of, 0)
                for b in range(nb):
                    vec[0, b] = start_ref[:, b * tile : (b + 1) * tile].astype(F32)
            inner(i - 2, 0, nb // 2)
        if i == stages + 2:
            eliminate(16, 40)
        if has(i - 3):
            share(i - 3)
        if has(i - 2):
            inner(i - 2, nb // 2, nb)
        if i == stages:
            sum_start(0, 1, sum_end(0, 0))
        if i == stages + 1:
            start_elimination(sum_end(0, 1))
            eliminate(0, 16)
        if i == stages + 2:
            eliminate(40, width)

    sum_start(1, 0, pack(ray[...]))
    linv = mat[...][:, width:]
    columns = group * tile

    def basis(first, last):
        for i in range(first, last):
            view = pl.ds(i * columns, columns)
            basis_vmem[:, view] = jnp.dot(
                linv, wide(fslot, i, slice(None)), precision=HIGHEST, preferred_element_type=F32
            )
            basis_copy(i).start()

    def basis_copy(i):
        view = pl.ds(i * columns, columns)
        return pltpu.make_async_copy(basis_vmem.at[:, view], basis_ref.at[:, view], basis_sem.at[i])

    groups = nb // group
    basis(0, groups // 2)
    sum_start(1, 1, sum_end(1, 0))
    basis(groups // 2, groups)
    rayleigh_t = unpack(sum_end(1, 1)) / rows_total
    proj_ref[...] = nt(nt(linv, rayleigh_t), linv)
    for i in range(groups):
        basis_copy(i).wait()


def body(start_block, tiles_in, tiles_out, in_cols, out_cols, export_list, recv_list):
    width, local_rows = start_block.shape
    nb, tp_in, tile, _ = tiles_in.shape
    tp_out = tiles_out.shape[1]
    count = (tp_in + tp_out) * tile
    devices = lax.axis_size("dom") * lax.axis_size("sub")
    kc = width // NC
    stages = OPS * NC
    blocks = nb * 4
    slots = recv_list.size
    hbm = pl.BlockSpec(memory_space=pl.ANY)
    vmem = pl.BlockSpec(memory_space=pltpu.VMEM)
    dma = pltpu.SemaphoreType.DMA
    return pl.pallas_call(
        functools.partial(
            kernel, local_rows * devices, 1.0 / (1.25 * math.sqrt(count)), count
        ),
        out_shape=(
            jax.ShapeDtypeStruct((width, local_rows), F32),
            jax.ShapeDtypeStruct((width, width), F32),
        ),
        in_specs=[hbm] * 7,
        out_specs=(hbm, vmem),
        scratch_shapes=[
            pltpu.VMEM(start_block.shape, BF16),
            pltpu.VMEM(tiles_in.shape, BF16),
            pltpu.VMEM(tiles_out.shape, BF16),
            *[pltpu.VMEM((blocks, kc, tile), BF16) for _ in range(3 * NC)],
            *[pltpu.VMEM((slots, kc, tile), BF16) for _ in range(2 * NC)],
            pltpu.VMEM((2, nb, width, tile), F32),
            pltpu.VMEM((NC, nb, kc, tile), F32),
            pltpu.VMEM((nb, 8, tile), F32),
            pltpu.VMEM((nb, 8, tile), F32),
            pltpu.VMEM((blocks, tile), F32),
            pltpu.SMEM((tp_in, nb), jnp.int32),
            pltpu.SMEM((tp_out, nb), jnp.int32),
            pltpu.SMEM((export_list.size,), jnp.int32),
            pltpu.SMEM(recv_list.shape[:1:-1], jnp.int32),
            pltpu.SMEM((tp_out, nb), jnp.int32),
            pltpu.VMEM((width, 2 * width), F32),
            pltpu.VMEM((width, width), F32),
            pltpu.VMEM((2, 8, width // 2, 2 * width), F32),
            pltpu.VMEM((2, 16, width // 2, 2 * width), F32),
            pltpu.VMEM((width, local_rows), F32),
            dma((4,)),
            dma,
            dma((8, 2)),
            dma,
            dma,
            dma((stages, 6)),
            dma((stages, 6)),
            dma((stages,)),
            dma((stages,)),
            dma((stages,)),
            dma((stages,)),
            dma((2, 2)),
            dma((2, 2)),
            dma((8,)),
        ],
        compiler_params=pltpu.CompilerParams(
            collective_id=0, has_side_effects=True, vmem_limit_bytes=60 << 20
        ),
        name="filtered_step",
    )(
        start_block, tiles_in, tiles_out, in_cols.T, out_cols.T,
        export_list.reshape(-1), recv_list[0, 0].T,
    )


def solution(mesh):
    return jax.shard_map(
        body,
        mesh=mesh,
        in_specs=(
            P(None, ("dom", "sub")),
            P(("dom", "sub"), None, None, None),
            P(("dom", "sub"), None, None, None),
            P(("dom", "sub"), None),
            P(("dom", "sub"), None),
            P("dom", "sub", None),
            P("dom", "sub", None, None),
        ),
        out_specs=(P(None, ("dom", "sub")), P()),
        check_vma=False,
    )
```

time: 159 us -> 136 us (0.86)
  Pallas kernels: 150 us -> 131 us
  local copies, waits for them, and re-layouts: 7.87 us -> 3.64 us
    pallas_call x1, Pallas kernels: 150 us -> 131 us  [body(): pl.pallas_call(functools.partial(kernel, local_rows * devices, 1.0 / (1.2...]
    unnamed x11 -> x2, local copies, waits for them, and re-layouts: 7.77 us -> 3.64 us
where the time goes in v2:
time: 136 us
  Pallas kernels  131 us (96%)
  local copies, waits for them, and re-layouts  3.64 us (3%)
    pallas_call x1, Pallas kernels, body(): pl.pallas_call(functools.partial(kernel, local_rows * devices, 1.0 / (1.2...  131 us
    unnamed x2, local copies, waits for them, and re-layouts  3.64 us

profile of v2, /device:TPU:1, one launch (start us, length us, event | category | flops | bytes accessed | tf_op | source)
XLA Modules:
  0.0 135.8 jit_solution(1158891281284387986)
XLA Ops:
  0.6 131.5 %filtered_step.1 = (f32[64,4096]{1,0:T(8,128)}, f32[64,64]{1,0:T(8,128)}) custom-call(bf16[64,4096]{1,0:T(8,128)(2,1)} %start_hbm.1, bf16[32,12,128,128]{3,2,1,0:T(8,128)(2,1)} %tin_hbm.1, bf16[32,4,128,128]{3,2,1,0:T(8,128)(2,1)} %tout_hbm.1, s32[12,32]{1,0:T(8,128)} %bitcast.6, s32[4,32]{1,0:T(4,128)} %bitcast.7, s32[4]{0:T(128)} %bitcast.9, s32[4,32]{1,0:T(4,128)} %bitcast.8), custom_call_target="tpu_custom_call" | custom-call | tf_op jit(solution)/shard_map/filtered_step/pallas_call | solution.py:422
  132.1 2.3 %copy.11 = f32[64,4096]{1,0:T(8,128)} copy(f32[64,4096]{1,0:T(8,128)} %get-tuple-element.4) | data formatting | bytes 2097152
  134.4 1.4 %copy.12 = f32[64,64]{1,0:T(8,128)} copy(f32[64,64]{1,0:T(8,128)} %get-tuple-element.5) | data formatting | bytes 32768

commit v3 on v2

--- a/solution.py
+++ b/solution.py
@@ -20,6 +20,19 @@
     return lax.dot_general(
         a, b, (((1,), (1,)), ((), ())), precision=HIGHEST, preferred_element_type=F32
     )
+
+
+def mul(a, b):
+    return jnp.dot(a, b, preferred_element_type=F32)
+
+
+def mul_nt(a, b):
+    return lax.dot_general(a, b, (((1,), (1,)), ((), ())), preferred_element_type=F32)
+
+
+def split(value):
+    high = value.astype(BF16)
+    return high, (value - high.astype(F32)).astype(BF16)
 
 
 def kernel(
@@ -33,7 +46,7 @@
     parts = [scratch[NC * p : NC * p + NC] for p in range(2)]
     scratch = scratch[2 * NC :]
     outs = [scratch[NC * p : NC * p + NC] for p in range(2)]
-    (vec, acc, dinv, rowf, dall, ic, oc, exp_ref, recv_ref, oidx, mat, ray, near, far, basis_vmem,
+    (vec, acc, dinv, rowf, dall, ic, oc, exp_ref, recv_ref, oidx, fil_high, fil_low, image, mat, ray, near, far, basis_vmem,
      table_sem, start_sem, load_sem, d_send, d_recv, y_send, y_recv, xz_send, xz_recv, core_send, core_recv,
      sum_send, sum_recv, basis_sem) = scratch[2 * NC :]
     width = start_ref.shape[0]
@@ -53,6 +66,7 @@
         return (zz * 8 + xx * 2 + cc, (s + dy) % 4)
 
     plane = [(dz, dx) for dz in range(4) for dx in range(4) if (dz, dx) != (0, 0)]
+    plane.sort(key=lambda d: -min(d[0], 4 - d[0]) - min(d[1], 4 - d[1]))
     right, left, partner = dev(0, 0, 1, 0), dev(0, 0, 3, 0), dev(0, 0, 0, 1)
 
     barrier = pltpu.get_barrier_semaphore()
@@ -161,14 +175,14 @@
         block = out.at[pl.ds(base, offered)]
         return [
             pltpu.make_async_remote_copy(
-                src_ref=block, dst_ref=block, send_sem=xz_send.at[j], recv_sem=xz_recv.at[j],
+                src_ref=block, dst_ref=block, send_sem=xz_send.at[j], recv_sem=xz_recv.at[j, (4 - dz) % 4],
                 device_id=dev(dz, dx, 0, 0), device_id_type=MESH,
             )
             for dz, dx in plane
         ]
 
-    def wait_bytes(out, sem):
-        view = out.at[pl.ds(0, len(plane) * offered)]
+    def wait_bytes(out, sem, n):
+        view = out.at[pl.ds(0, n * offered)]
         pltpu.make_async_copy(view, view, sem).wait()
 
     def export(j):
@@ -193,18 +207,20 @@
         for cp in xz_copies(j):
             cp.start()
 
-    def core_copy(j):
-        block = outs[(j // NC) % 2][j % NC].at[pl.ds(core * (16 * offered), 16 * offered)]
+    def core_copy(j, dz):
+        row = core * (16 * offered) + ((z + dz) % 4) * (4 * offered)
+        block = outs[(j // NC) % 2][j % NC].at[pl.ds(row, 4 * offered)]
         return pltpu.make_async_remote_copy(
-            src_ref=block, dst_ref=block, send_sem=core_send.at[j], recv_sem=core_recv.at[j],
+            src_ref=block, dst_ref=block, send_sem=core_send.at[j, dz], recv_sem=core_recv.at[j, dz],
             device_id=partner, device_id_type=MESH,
         )
 
     def share(j):
         out = outs[(j // NC) % 2][j % NC]
-        wait_bytes(out, xz_recv.at[j])
-        core_copy(j).start()
-        wait_bytes(out, xz_send.at[j])
+        for dz in (0, 1, 3, 2):
+            wait_bytes(out, xz_recv.at[j, dz], 3 if dz == 0 else 4)
+            core_copy(j, dz).start()
+        wait_bytes(out, xz_send.at[j], len(plane))
         for cp in y_copies(j)[1]:
             cp.wait_send()
 
@@ -223,8 +239,9 @@
 
     def outer(j):
         n, c = j // NC, j % NC
-        core_copy(j).wait_recv()
-        core_copy(j).wait_send()
+        for dz in range(4):
+            core_copy(j, dz).wait_recv()
+            core_copy(j, dz).wait_send()
         out = outs[n % 2][c]
         rows = pl.ds(c * kc, kc)
         p = (n + 1) % 2
@@ -233,35 +250,31 @@
             v = jnp.concatenate([out[oidx[t, b]] for t in range(tp_out)], axis=1)
             o = acc[c, b] + jnp.dot(v, tout[b].reshape(tp_out * tile, tile), preferred_element_type=F32)
             new = o * rowf[b, :1, :]
-            if n in (1, 2):
-                new = 2.0 * new - vec[p, b, rows, :]
-            vec[p, b, rows, :] = new
+            columns = pl.ds(pl.multiple_of(b * tile, tile), tile)
+            if n == 0:
+                vec[b, rows, :] = new
+            elif n == 1:
+                new = 2.0 * new - start_ref[rows, columns].astype(F32)
+            elif n == 2:
+                new = 2.0 * new - vec[b, rows, :]
+                fil_high[rows, columns], fil_low[rows, columns] = split(new)
+            else:
+                image[:kc, columns], image[kc:, columns] = split(new)
             if n + 1 < OPS:
                 scale(parts[p][c], c, b, new)
             return carry
 
         lax.fori_loop(0, nb, one, 0, unroll=8)
 
-    fslot = OPS % 2 ^ 1
-    group = 4
-
-    def wide(slot, i, rows):
-        return jnp.concatenate([vec[slot, i * group + k, rows, :] for k in range(group)], axis=1)
-
-    def product(slot):
-        def one(i, carry):
-            return carry + nt(wide(slot, i, slice(None)), wide(fslot, i, slice(None)))
-
-        zero = jnp.zeros((width, width), F32)
-        return lax.fori_loop(0, nb // group, one, zero)
+    def product():
+        high = fil_high[...]
+        both = mul_nt(high, jnp.concatenate([high, fil_low[...]], axis=0))
+        return both[:, :width] + both[:, width:] + mul_nt(fil_low[...], high)
 
     def rayleigh(j):
-        rows = pl.ds((j % NC) * kc, kc)
-
-        def one(i, carry):
-            return carry + nt(wide(1 - fslot, i, rows), wide(fslot, i, slice(None)))
-
-        ray[rows, :] = lax.fori_loop(0, nb // group, one, jnp.zeros((kc, width), F32))
+        both = mul_nt(image[...], fil_high[...])
+        got = both[:kc] + both[kc:] + mul_nt(image[:kc, :], fil_low[...])
+        ray[pl.ds((j % NC) * kc, kc), :] = got
 
     def spread(use, k):
         buf = (near, far)[k].at[use]
@@ -347,6 +360,7 @@
     for cp in degree_copies():
         cp.start()
     send_own(3, 2)
+    lax.fori_loop(0, nb * tp_out, slot_of, 0, unroll=8)
     degrees_end()
     for i in range(2, stages + NC):
         if has(i - 4):
@@ -358,52 +372,66 @@
         if i == stages:
             forward(i - 1)
         if i == stages - 1:
-            sum_start(0, 0, pack(product(fslot)))
+            sum_start(0, 0, pack(product()))
         if has(i - 2):
             export(i - 2)
-            if i == 2:
-                lax.fori_loop(0, nb * tp_out, slot_of, 0)
-                for b in range(nb):
-                    vec[0, b] = start_ref[:, b * tile : (b + 1) * tile].astype(F32)
             inner(i - 2, 0, nb // 2)
-        if i == stages + 2:
-            eliminate(16, 40)
         if has(i - 3):
             share(i - 3)
         if has(i - 2):
             inner(i - 2, nb // 2, nb)
-        if i == stages:
+        if i == stages - 1:
             sum_start(0, 1, sum_end(0, 0))
-        if i == stages + 1:
-            start_elimination(sum_end(0, 1))
-            eliminate(0, 16)
-        if i == stages + 2:
-            eliminate(40, width)
 
     sum_start(1, 0, pack(ray[...]))
+    start_elimination(sum_end(0, 1))
+    eliminate(0, 40)
+    sum_start(1, 1, sum_end(1, 0))
+    eliminate(40, width)
     linv = mat[...][:, width:]
-    columns = group * tile
+    linv_high, linv_low = split(linv)
+    linv_both = jnp.concatenate([linv_high, linv_low], axis=0)
+    columns = 4 * tile
 
     def basis(first, last):
         for i in range(first, last):
             view = pl.ds(i * columns, columns)
-            basis_vmem[:, view] = jnp.dot(
-                linv, wide(fslot, i, slice(None)), precision=HIGHEST, preferred_element_type=F32
-            )
+            both = mul(linv_both, fil_high[:, view])
+            basis_vmem[:, view] = both[:width] + both[width:] + mul(linv_high, fil_low[:, view])
             basis_copy(i).start()
 
     def basis_copy(i):
         view = pl.ds(i * columns, columns)
         return pltpu.make_async_copy(basis_vmem.at[:, view], basis_ref.at[:, view], basis_sem.at[i])
 
-    groups = nb // group
-    basis(0, groups // 2)
-    sum_start(1, 1, sum_end(1, 0))
-    basis(groups // 2, groups)
+    groups = nb // 4
+    basis(0, groups)
     rayleigh_t = unpack(sum_end(1, 1)) / rows_total
     proj_ref[...] = nt(nt(linv, rayleigh_t), linv)
     for i in range(groups):
         basis_copy(i).wait()
+
+
+def deliver(basis, proj, basis_out, proj_out, held, held_proj, sem):
+    width = basis.shape[1] // 4
+    steps = []
+    for i in range(5):
+        if i < 4:
+            part = (slice(None), pl.ds(i * width, width))
+            refs = basis.at[part], held.at[part], basis_out.at[part]
+        else:
+            refs = proj, held_proj, proj_out
+        steps.append(
+            (pltpu.make_async_copy(refs[0], refs[1], sem.at[i, 0]),
+             pltpu.make_async_copy(refs[1], refs[2], sem.at[i, 1]))
+        )
+    for come, _ in steps:
+        come.start()
+    for come, go in steps:
+        come.wait()
+        go.start()
+    for _, go in steps:
+        go.wait()
 
 
 def body(start_block, tiles_in, tiles_out, in_cols, out_cols, export_list, recv_list):
@@ -419,7 +447,7 @@
     hbm = pl.BlockSpec(memory_space=pl.ANY)
     vmem = pl.BlockSpec(memory_space=pltpu.VMEM)
     dma = pltpu.SemaphoreType.DMA
-    return pl.pallas_call(
+    outputs = pl.pallas_call(
         functools.partial(
             kernel, local_rows * devices, 1.0 / (1.25 * math.sqrt(count)), count
         ),
@@ -435,7 +463,7 @@
             pltpu.VMEM(tiles_out.shape, BF16),
             *[pltpu.VMEM((blocks, kc, tile), BF16) for _ in range(3 * NC)],
             *[pltpu.VMEM((slots, kc, tile), BF16) for _ in range(2 * NC)],
-            pltpu.VMEM((2, nb, width, tile), F32),
+            pltpu.VMEM((nb, width, tile), F32),
             pltpu.VMEM((NC, nb, kc, tile), F32),
             pltpu.VMEM((nb, 8, tile), F32),
             pltpu.VMEM((nb, 8, tile), F32),
@@ -445,6 +473,9 @@
             pltpu.SMEM((export_list.size,), jnp.int32),
             pltpu.SMEM(recv_list.shape[:1:-1], jnp.int32),
             pltpu.SMEM((tp_out, nb), jnp.int32),
+            pltpu.VMEM((width, local_rows), BF16),
+            pltpu.VMEM((width, local_rows), BF16),
+            pltpu.VMEM((2 * kc, local_rows), BF16),
             pltpu.VMEM((width, 2 * width), F32),
             pltpu.VMEM((width, width), F32),
             pltpu.VMEM((2, 8, width // 2, 2 * width), F32),
@@ -458,9 +489,9 @@
             dma((stages, 6)),
             dma((stages, 6)),
             dma((stages,)),
-            dma((stages,)),
-            dma((stages,)),
-            dma((stages,)),
+            dma((stages, 4)),
+            dma((stages, 4)),
+            dma((stages, 4)),
             dma((2, 2)),
             dma((2, 2)),
             dma((8,)),
@@ -473,6 +504,15 @@
         start_block, tiles_in, tiles_out, in_cols.T, out_cols.T,
         export_list.reshape(-1), recv_list[0, 0].T,
     )
+    return pl.pallas_call(
+        deliver,
+        out_shape=tuple(jax.ShapeDtypeStruct(o.shape, o.dtype) for o in outputs),
+        in_specs=[hbm, hbm],
+        out_specs=(hbm, hbm),
+        scratch_shapes=[*[pltpu.VMEM(o.shape, o.dtype) for o in outputs], dma((5, 2))],
+        compiler_params=pltpu.CompilerParams(vmem_limit_bytes=60 << 20),
+        name="deliver",
+    )(*outputs)
 
 
 def solution(mesh):

time: 136 us -> 128 us (0.941)
  Pallas kernels: 131 us -> 127 us
  local copies, waits for them, and re-layouts: 3.64 us -> 0 us
    pallas_call x1, Pallas kernels: 131 us -> 125 us  [body(): pl.pallas_call(functools.partial(kernel, local_rows * devices, 1.0 / (1.2...]
    unnamed x2 -> x0, local copies, waits for them, and re-layouts: 3.64 us -> none
    pallas_call x0 -> x1, Pallas kernels: none -> 2 us  [body(): pl.pallas_call(deliver, out_shape=tuple((jax.ShapeDtypeStruct(o.shape, o....]
where the time goes in v3:
time: 128 us
  Pallas kernels  127 us (99%)
    pallas_call x1, Pallas kernels, body(): pl.pallas_call(functools.partial(kernel, local_rows * devices, 1.0 / (1.2...  125 us

profile of v3, /device:TPU:1, one launch (start us, length us, event | category | flops | bytes accessed | tf_op | source)
XLA Modules:
  0.0 127.9 jit_solution(9011800873001722338)
XLA Ops:
  0.6 125.1 %filtered_step.1 = (f32[64,4096]{1,0:T(8,128)}, f32[64,64]{1,0:T(8,128)}) custom-call(bf16[64,4096]{1,0:T(8,128)(2,1)} %start_hbm.1, bf16[32,12,128,128]{3,2,1,0:T(8,128)(2,1)} %tin_hbm.1, bf16[32,4,128,128]{3,2,1,0:T(8,128)(2,1)} %tout_hbm.1, s32[12,32]{1,0:T(8,128)} %bitcast.6, s32[4,32]{1,0:T(4,128)} %bitcast.7, s32[4]{0:T(128)} %bitcast.9, s32[4,32]{1,0:T(4,128)} %bitcast.8), custom_call_target="tpu_custom_call" | custom-call | tf_op jit(solution)/shard_map/filtered_step/pallas_call | solution.py:450
  125.7 2.0 %deliver.1 = (f32[64,4096]{1,0:T(8,128)}, f32[64,64]{1,0:T(8,128)}) custom-call(f32[64,4096]{1,0:T(8,128)} %get-tuple-element.4.basis, f32[64,64]{1,0:T(8,128)} %get-tuple-element.5.proj), custom_call_target="tpu_custom_call" | custom-call | tf_op jit(solution)/shard_map/deliver/pallas_call | solution.py:507

commit v4 on v3

--- a/solution.py
+++ b/solution.py
@@ -155,14 +155,10 @@
         forwards = [cp(4, lo, right), cp(5, hi + half, left)]
         return sends, forwards
 
-    def send_own(j, later=None):
+    def send_own(j, which=(0, 1, 2, 3)):
         sends = y_copies(j)[0]
-        sends[0].start()
-        sends[1].start()
-        if later is not None:
-            forward(later)
-        sends[2].start()
-        sends[3].start()
+        for k in which:
+            sends[k].start()
 
     def forward(j):
         sends, forwards = y_copies(j)
@@ -232,16 +228,18 @@
             acc[c, b] = jnp.dot(v, tin[b].reshape(tp_in * tile, tile), preferred_element_type=F32)
             return carry
 
-        lax.fori_loop(first, last, one, 0, unroll=8)
+        lax.fori_loop(first, last, one, 0, unroll=16)
 
     def scale(part, c, b, new):
         part[own + b] = (new * dinv[b, :1, :]).astype(BF16)
 
-    def outer(j):
-        n, c = j // NC, j % NC
+    def shared(j):
         for dz in range(4):
             core_copy(j, dz).wait_recv()
             core_copy(j, dz).wait_send()
+
+    def outer(j, first, last):
+        n, c = j // NC, j % NC
         out = outs[n % 2][c]
         rows = pl.ds(c * kc, kc)
         p = (n + 1) % 2
@@ -264,7 +262,7 @@
                 scale(parts[p][c], c, b, new)
             return carry
 
-        lax.fori_loop(0, nb, one, 0, unroll=8)
+        lax.fori_loop(first, last, one, 0, unroll=16)
 
     def product():
         high = fil_high[...]
@@ -353,35 +351,46 @@
     for cp in table_copies:
         cp.wait()
     degrees(0, 3)
-    send_own(1, 0)
+    send_own(1, (0, 1))
+    forward(0)
+    send_own(1, (2, 3))
     degrees(3, 6)
-    send_own(2, 1)
+    send_own(2, (0, 1))
+    forward(1)
+    send_own(2, (2, 3))
     degrees(6, pieces)
     for cp in degree_copies():
         cp.start()
-    send_own(3, 2)
+    send_own(3, (0, 1))
+    forward(2)
+    send_own(3, (2, 3))
     lax.fori_loop(0, nb * tp_out, slot_of, 0, unroll=8)
     degrees_end()
+    export(0)
     for i in range(2, stages + NC):
         if has(i - 4):
-            outer(i - 4)
+            shared(i - 4)
+            outer(i - 4, 0, half)
+        if i >= NC and has(i - 1):
+            forward(i - 1)
+        if i >= NC and has(i):
+            send_own(i, (0,))
+        if has(i - 4):
+            outer(i - 4, half, nb)
+        if i >= NC and has(i):
+            send_own(i, (1, 2, 3))
         if i - 4 >= stages - NC:
             rayleigh(i - 4)
-        if i >= NC and has(i):
-            send_own(i, i - 1)
-        if i == stages:
-            forward(i - 1)
+        if has(i - 3):
+            share(i - 3)
         if i == stages - 1:
             sum_start(0, 0, pack(product()))
+        if i == stages:
+            sum_start(0, 1, sum_end(0, 0))
         if has(i - 2):
-            export(i - 2)
-            inner(i - 2, 0, nb // 2)
-        if has(i - 3):
-            share(i - 3)
-        if has(i - 2):
-            inner(i - 2, nb // 2, nb)
-        if i == stages - 1:
-            sum_start(0, 1, sum_end(0, 0))
+            inner(i - 2, 0, nb)
+        if has(i - 1):
+            export(i - 1)
 
     sum_start(1, 0, pack(ray[...]))
     start_elimination(sum_end(0, 1))

time: 128 us -> 122 us (0.953)
  Pallas kernels: 127 us -> 121 us
    pallas_call x1, Pallas kernels: 125 us -> 119 us  [body(): pl.pallas_call(functools.partial(kernel, local_rows * devices, 1.0 / (1.2...]
where the time goes in v4:
time: 122 us
  Pallas kernels  121 us (99%)
    pallas_call x1, Pallas kernels, body(): pl.pallas_call(functools.partial(kernel, local_rows * devices, 1.0 / (1.2...  119 us

profile of v4, /device:TPU:1, one launch (start us, length us, event | category | flops | bytes accessed | tf_op | source)
XLA Modules:
  0.0 122.2 jit_solution(17032742937274168029)
XLA Ops:
  0.6 119.4 %filtered_step.1 = (f32[64,4096]{1,0:T(8,128)}, f32[64,64]{1,0:T(8,128)}) custom-call(bf16[64,4096]{1,0:T(8,128)(2,1)} %start_hbm.1, bf16[32,12,128,128]{3,2,1,0:T(8,128)(2,1)} %tin_hbm.1, bf16[32,4,128,128]{3,2,1,0:T(8,128)(2,1)} %tout_hbm.1, s32[12,32]{1,0:T(8,128)} %bitcast.6, s32[4,32]{1,0:T(4,128)} %bitcast.7, s32[4]{0:T(128)} %bitcast.9, s32[4,32]{1,0:T(4,128)} %bitcast.8), custom_call_target="tpu_custom_call" | custom-call | tf_op jit(solution)/shard_map/filtered_step/pallas_call | solution.py:459
  120.0 2.0 %deliver.1 = (f32[64,4096]{1,0:T(8,128)}, f32[64,64]{1,0:T(8,128)}) custom-call(f32[64,4096]{1,0:T(8,128)} %get-tuple-element.4.basis, f32[64,64]{1,0:T(8,128)} %get-tuple-element.5.proj), custom_call_target="tpu_custom_call" | custom-call | tf_op jit(solution)/shard_map/deliver/pallas_call | solution.py:516

commit v5 on v4

--- a/solution.py
+++ b/solution.py
@@ -104,8 +104,7 @@
         return carry
 
     def total(ref, b, n):
-        a = jnp.abs(ref[b].reshape(n * tile, tile)).astype(F32)
-        return jnp.sum(a.reshape(n * tile // 8, 8, tile), axis=0)
+        return mul(jnp.ones((16, n * tile), BF16), jnp.abs(ref[b].reshape(n * tile, tile)))
 
     def degrees(first, last):
         for i in range(first, last):
@@ -113,7 +112,7 @@
                 cp.wait()
 
             def degree(b, carry):
-                mag = jnp.sum(total(tin, b, tp_in) + total(tout, b, tp_out), axis=0, keepdims=True)
+                mag = (total(tin, b, tp_in) + total(tout, b, tp_out))[:1]
                 inv = 1.0 / jnp.sqrt(mag / count + 1e-06)
                 dall[pl.ds(own + b, 1), :] = inv
                 dinv[b] = jnp.broadcast_to(inv, (8, tile))
@@ -381,6 +380,8 @@
             send_own(i, (1, 2, 3))
         if i - 4 >= stages - NC:
             rayleigh(i - 4)
+        if i == 3:
+            inner(1, 0, half)
         if has(i - 3):
             share(i - 3)
         if i == stages - 1:
@@ -388,7 +389,7 @@
         if i == stages:
             sum_start(0, 1, sum_end(0, 0))
         if has(i - 2):
-            inner(i - 2, 0, nb)
+            inner(i - 2, half if i == 3 else 0, nb)
         if has(i - 1):
             export(i - 1)
 

time: 122 us -> 122 us (level)
  no operation moved by 1% of the time
where the time goes in v5:
time: 122 us
  Pallas kernels  121 us (99%)
    pallas_call x1, Pallas kernels, body(): pl.pallas_call(functools.partial(kernel, local_rows * devices, 1.0 / (1.2...  119 us

profile of v5, /device:TPU:1, one launch (start us, length us, event | category | flops | bytes accessed | tf_op | source)
XLA Modules:
  0.0 121.9 jit_solution(701171124158806357)
XLA Ops:
  0.6 119.0 %filtered_step.1 = (f32[64,4096]{1,0:T(8,128)}, f32[64,64]{1,0:T(8,128)}) custom-call(bf16[64,4096]{1,0:T(8,128)(2,1)} %start_hbm.1, bf16[32,12,128,128]{3,2,1,0:T(8,128)(2,1)} %tin_hbm.1, bf16[32,4,128,128]{3,2,1,0:T(8,128)(2,1)} %tout_hbm.1, s32[12,32]{1,0:T(8,128)} %bitcast.6, s32[4,32]{1,0:T(4,128)} %bitcast.7, s32[4]{0:T(128)} %bitcast.9, s32[4,32]{1,0:T(4,128)} %bitcast.8), custom_call_target="tpu_custom_call" | custom-call | tf_op jit(solution)/shard_map/filtered_step/pallas_call | solution.py:460
  119.7 2.0 %deliver.1 = (f32[64,4096]{1,0:T(8,128)}, f32[64,64]{1,0:T(8,128)}) custom-call(f32[64,4096]{1,0:T(8,128)} %get-tuple-element.4.basis, f32[64,64]{1,0:T(8,128)} %get-tuple-element.5.proj), custom_call_target="tpu_custom_call" | custom-call | tf_op jit(solution)/shard_map/deliver/pallas_call | solution.py:517
